TPU v7x, 128 devices: a whole 4x4x4 slice. The times are simulated.
128 devices in a mesh: dp: 32 (over x_lo, z, y), seq: 4 (over x_hi, core).
Axes of the slice: x: 4 (x_hi: 2, x_lo: 2; x = x_hi * 2 + x_lo), y: 4, z: 4, core: 2. Of those that a mesh axis runs over, the one named last changes fastest.
Arguments:
- latents: bfloat16 [65536, 3072], P(('dp', 'seq')), may hold values from -6 to 6
- target: int32 [65536], P(('dp', 'seq')), may hold values from 0 to 65535, as said below
- segment_ids: int32 [32, 2048], P('dp', 'seq'), may hold values from 0 to 7, never falling along the last dimension, each value on 1 to 512 neighbouring positions
- clip_bucket: int32 [32, 8], P('dp'), may hold values from 0 to 15
- mod_table: bfloat16 [16, 6144], replicated, may hold values from -3 to 3
- w_query: bfloat16 [3072, 1536], P('dp', 'seq')
- w_key: bfloat16 [3072, 1536], P('dp', 'seq')
- w_value: bfloat16 [3072, 1536], P('dp', 'seq'), may hold values from -0.109375 to 0.109375
Outputs:
- attended: bfloat16 [65536, 1536], P(('dp', 'seq'))
Inputs may be any that keep to these rules, and one draw needn't show every extreme that they name: `target`: a permutation of 0 to 65535; a token stays at the same index of seq; a device sends at most 24 tokens to one index of dp, exactly 24 to some index in every draw, and sends to at most (535) // 24 + 1 indices.
All inputs are finite; a program needn't handle non-finite values.
Results may differ from a plain program's by a relative error of at most 0.0051.
Values may be sent and summed in bfloat16 or wider, within the bound.
A program may use at most 128 MiB of HBM per device.

v0:
```python
import jax
import jax.numpy as jnp
from jax import lax
from jax.sharding import PartitionSpec as P

HEAD_DIM = 128


def modulated_norm(latent_rows, segment_row, bucket_row, mod_table):
    clip_count = bucket_row.shape[0]
    bucket_count = mod_table.shape[0]
    width = latent_rows.shape[1]
    clip_hit = segment_row[:, None] == jnp.arange(clip_count, dtype=jnp.int32)[None, :]
    token_bucket = jnp.sum(jnp.where(clip_hit, bucket_row[None, :], 0), axis=1)
    bucket_hit = (
        token_bucket[:, None] == jnp.arange(bucket_count, dtype=jnp.int32)[None, :]
    ).astype(jnp.bfloat16)
    modulation = jnp.dot(bucket_hit, mod_table, preferred_element_type=jnp.float32)
    shift_part = modulation[:, :width]
    scale_part = modulation[:, width:]
    widened = latent_rows.astype(jnp.float32)
    row_mean = jnp.mean(widened, axis=1, keepdims=True)
    centered = widened - row_mean
    row_var = jnp.mean(centered * centered, axis=1, keepdims=True)
    normalized = centered * lax.rsqrt(row_var + 1e-06)
    return (normalized * (1.0 + scale_part) + shift_part).astype(jnp.bfloat16)


def project_three(hidden_rows, pieces):
    return (
        jnp.dot(hidden_rows, pieces[0], preferred_element_type=jnp.float32),
        jnp.dot(hidden_rows, pieces[1], preferred_element_type=jnp.float32),
        jnp.dot(hidden_rows, pieces[2], preferred_element_type=jnp.float32),
    )


def attend(query_rows, key_rows, value_rows, sequence_clips):
    length = query_rows.shape[0]
    heads_here = query_rows.shape[1] // HEAD_DIM
    block_rows = min(512, length)
    block_count = length // block_rows
    factor = HEAD_DIM ** (-0.5)
    query_blocks = query_rows.reshape(block_count, block_rows, heads_here, HEAD_DIM)
    clip_blocks = sequence_clips.reshape(block_count, block_rows)
    key_heads = key_rows.reshape(length, heads_here, HEAD_DIM)
    value_heads = value_rows.reshape(length, heads_here, HEAD_DIM)

    def attend_block(blocks):
        query_block, clip_block = blocks
        scores = (
            jnp.einsum("qhd,khd->hqk", query_block, key_heads, preferred_element_type=jnp.float32)
            * factor
        )
        same_clip = clip_block[:, None] == sequence_clips[None, :]
        scores = jnp.where(same_clip[None, :, :], scores, -1e30)
        row_max = jnp.max(scores, axis=2, keepdims=True)
        exponent = jnp.exp(scores - row_max)
        row_total = jnp.sum(exponent, axis=2, keepdims=True)
        weights_bf = (exponent / row_total).astype(jnp.bfloat16)
        result = jnp.einsum(
            "hqk,khd->qhd", weights_bf, value_heads, preferred_element_type=jnp.float32
        )
        return result.reshape(block_rows, heads_here * HEAD_DIM).astype(jnp.bfloat16)

    outcome = lax.map(attend_block, (query_blocks, clip_blocks))
    return outcome.reshape(length, heads_here * HEAD_DIM)


def on_device(latents, target, segment_ids, clip_bucket, mod_table, w_query, w_key, w_value):
    local_rows = latents.shape[0]
    width = latents.shape[1]
    group_count = lax.axis_size("dp")
    seq_count = lax.axis_size("seq")
    capacity = max(2, 3 * local_rows // (2 * group_count))
    dest_device = target // (seq_count * local_rows)
    dest_row = target % local_rows
    device_hit = (dest_device[:, None] == jnp.arange(group_count, dtype=jnp.int32)[None, :]).astype(
        jnp.int32
    )
    earlier = jnp.cumsum(device_hit, axis=0) - device_hit
    rank_row = jnp.sum(earlier * device_hit, axis=1)
    send_slot = dest_device * capacity + rank_row
    outgoing = jnp.zeros((group_count * capacity, width), jnp.bfloat16).at[send_slot].set(latents)
    outgoing_rows = (
        jnp.full((group_count * capacity,), local_rows, jnp.int32).at[send_slot].set(dest_row)
    )
    incoming, incoming_rows = (
        lax.all_to_all(outgoing, "dp", split_axis=0, concat_axis=0, tiled=True),
        lax.all_to_all(outgoing_rows, "dp", split_axis=0, concat_axis=0, tiled=True),
    )
    placed = (
        jnp.zeros((local_rows, width), jnp.bfloat16).at[incoming_rows].set(incoming, mode="drop")
    )
    hidden = modulated_norm(placed, segment_ids[0], clip_bucket[0], mod_table)
    columns_full = (
        lax.all_gather(w_query, "seq", axis=1, tiled=True),
        lax.all_gather(w_key, "seq", axis=1, tiled=True),
        lax.all_gather(w_value, "seq", axis=1, tiled=True),
    )
    query_f, key_f, value_f = project_three(
        hidden,
        (
            lax.all_gather(columns_full[0], "dp", axis=0, tiled=True),
            lax.all_gather(columns_full[1], "dp", axis=0, tiled=True),
            lax.all_gather(columns_full[2], "dp", axis=0, tiled=True),
        ),
    )
    query_rows, key_rows, value_rows = (
        lax.all_to_all(
            query_f.astype(jnp.bfloat16), "seq", split_axis=1, concat_axis=0, tiled=True
        ),
        lax.all_to_all(key_f.astype(jnp.bfloat16), "seq", split_axis=1, concat_axis=0, tiled=True),
        lax.all_to_all(
            value_f.astype(jnp.bfloat16), "seq", split_axis=1, concat_axis=0, tiled=True
        ),
    )
    sequence_clips = lax.all_gather(segment_ids, "seq", axis=1, tiled=True)[0]
    head_output = attend(query_rows, key_rows, value_rows, sequence_clips)
    return lax.all_to_all(head_output, "seq", split_axis=0, concat_axis=1, tiled=True)


def solution(mesh):
    in_specs = (
        P(("dp", "seq"), None),
        P(("dp", "seq")),
        P("dp", "seq"),
        P("dp", None),
        P(),
        P("dp", "seq"),
        P("dp", "seq"),
        P("dp", "seq"),
    )
    out_specs = P(("dp", "seq"), None)
    return jax.shard_map(
        on_device, mesh=mesh, in_specs=in_specs, out_specs=out_specs, check_vma=False
    )
```

profile of v0, /device:TPU:1, one launch (start us, length us, event | category | flops | bytes accessed | tf_op | source)
XLA Modules:
  0.0 754.8 jit_solution(5516558058506112569)
XLA Ops:
  6.5 10.5 %all_gather.24 = bf16[96,1536]{1,0:T(8,128)(2,1)} all-gather(bf16[96,384]{1,0:T(8,128)(2,1)} %param.16), channel_id=1, replica_groups=mesh['dp'=32,'seq'=4] {'seq'}, dimensions={1}, use_global_device_ids=true | all-gather | bytes 368640 | tf_op jit(solution)/shard_map/all_gather | solution.py:97
  17.1 8.5 %all_gather.26 = bf16[96,1536]{1,0:T(8,128)(2,1)} all-gather(bf16[96,384]{1,0:T(8,128)(2,1)} %param.17), channel_id=1, replica_groups=mesh['dp'=32,'seq'=4] {'seq'}, dimensions={1}, use_global_device_ids=true | all-gather | bytes 368640 | tf_op jit(solution)/shard_map/all_gather | solution.py:98
  25.7 9.8 %all_gather.22 = bf16[96,1536]{1,0:T(8,128)(2,1)} all-gather(bf16[96,384]{1,0:T(8,128)(2,1)} %param.15), channel_id=1, replica_groups=mesh['dp'=32,'seq'=4] {'seq'}, dimensions={1}, use_global_device_ids=true | all-gather | bytes 368640 | tf_op jit(solution)/shard_map/all_gather | solution.py:96
  41.0 8.2 %all-to-all-start = ((s32[32,24,1]{1,2,0:T(1,128)}), s32[32,24,1]{1,2,0:T(1,128)S(1)}, u32[]{:S(2)}, u32[]{:S(2)}) async-start(s32[32,24,1]{1,2,0:T(1,128)} %bitcast.7), calls=%async_computation | async-start | bytes 32768 | tf_op jit(solution)/shard_map/all_to_all | solution.py:89
  49.2 9.0 %scatter_custom_fusion.1 = bf16[768,3072]{1,0:T(8,128)(2,1)} fusion(s32[512]{0:T(512)S(1)} %compare_select_fusion.1, bf16[512,3072]{1,0:T(8,128)(2,1)} %param.10, bf16[]{:T(256)} %constant.62.clone.1), kind=kCustom, calls=%fused_computation.38 | custom fusion | bytes 4719104 | tf_op jit(solution)/shard_map/scatter | solution.py:83
  58.2 8.2 %all-to-all-start.1 = ((bf16[32,24,3072]{2,1,0:T(8,128)(2,1)}), bf16[32,24,3072]{2,1,0:T(8,128)(2,1)}, u32[]{:S(2)}, u32[]{:S(2)}) async-start(bf16[32,24,3072]{2,1,0:T(8,128)(2,1)} %bitcast.87), calls=%async_computation.1 | async-start | bytes 9437184 | tf_op jit(solution)/shard_map/all_to_all | solution.py:88
  66.5 6.4 fusion.36
  74.2 85.9 %all-to-all-done.1 = bf16[32,24,3072]{2,1,0:T(8,128)(2,1)} async-done(((bf16[32,24,3072]{2,1,0:T(8,128)(2,1)}), bf16[32,24,3072]{2,1,0:T(8,128)(2,1)}, u32[]{:S(2)}, u32[]{:S(2)}) %all-to-all-start.1) | async-done | bytes 4718624 | tf_op jit(solution)/shard_map/all_to_all | solution.py:88
  160.1 11.7 %scatter_custom_fusion.2 = bf16[512,3072]{1,0:T(8,128)(2,1)S(1)} fusion(s32[768]{0:T(1024)S(1)} %fusion.42, bf16[768,3072]{1,0:T(8,128)(2,1)} %bitcast.9, bf16[]{:T(256)} %constant.62.clone.1), kind=kCustom, calls=%fused_computation.41 | custom fusion | bytes 3146240 | tf_op jit(solution)/shard_map/scatter | solution.py:92
  173.2 7.1 fusion.31
  180.3 41.6 %all-gather.6.cloned.1.call-done = bf16[3072,1536]{1,0:T(8,128)(2,1)} async-done(((bf16[96,1536]{1,0:T(8,128)(2,1)}), bf16[3072,1536]{1,0:T(8,128)(2,1)}) %all-gather.6.cloned.1.call-update) | async-done | bytes 9437200 | tf_op jit(solution)/shard_map/all_gather | solution.py:104
  221.9 9.4 %convolution_convert_fusion.1 = bf16[512,1536]{1,0:T(8,128)(2,1)S(1)} fusion(bf16[512,3072]{1,0:T(8,128)(2,1)} %fusion.31, bf16[3072,1536]{1,0:T(8,128)(2,1)} %all-gather.6.cloned.1.call-done), kind=kOutput, calls=%fused_computation.36 | convolution fusion | flops 4832624640 | bytes 14155776 | tf_op jit(solution)/shard_map/dot_general | solution.py:32
  232.9 19.1 %all-to-all-start.3 = ((bf16[512,4,384]{0,2,1:T(8,128)(2,1)}), bf16[512,4,384]{0,2,1:T(8,128)(2,1)S(1)}, u32[]{:S(2)}, u32[]{:S(2)}) async-start(bf16[512,4,384]{0,2,1:T(8,128)(2,1)} %bitcast.15), calls=%async_computation.3 | async-start | bytes 3145728 | tf_op jit(solution)/shard_map/all_to_all | solution.py:112
  252.0 147.3 %all-gather.8.cloned.1.call-done = bf16[3072,1536]{1,0:T(8,128)(2,1)} async-done(((bf16[96,1536]{1,0:T(8,128)(2,1)}), bf16[3072,1536]{1,0:T(8,128)(2,1)}) %all-gather.8.cloned.1.call-update) | async-done | bytes 9437200 | tf_op jit(solution)/shard_map/all_gather | solution.py:105
  399.3 9.4 %convolution_convert_fusion = bf16[512,1536]{1,0:T(8,128)(2,1)S(1)} fusion(bf16[512,3072]{1,0:T(8,128)(2,1)} %fusion.31, bf16[3072,1536]{1,0:T(8,128)(2,1)} %all-gather.8.cloned.1.call-done), kind=kOutput, calls=%fused_computation.35 | convolution fusion | flops 4832624640 | bytes 14155776 | tf_op jit(solution)/shard_map/dot_general | solution.py:33
  410.0 22.3 %all-to-all-start.4 = ((bf16[512,4,384]{2,0,1:T(8,128)(2,1)}), bf16[512,4,384]{2,0,1:T(8,128)(2,1)S(1)}, u32[]{:S(2)}, u32[]{:S(2)}) async-start(bf16[512,4,384]{2,0,1:T(8,128)(2,1)} %bitcast.92), calls=%async_computation.4 | async-start | bytes 3145728 | tf_op jit(solution)/shard_map/all_to_all | solution.py:113
  432.3 145.1 %all-gather.4.cloned.1.call-done = bf16[3072,1536]{1,0:T(8,128)(2,1)} async-done(((bf16[96,1536]{1,0:T(8,128)(2,1)}), bf16[3072,1536]{1,0:T(8,128)(2,1)}) %all-gather.4.cloned.1.call-update) | async-done | bytes 9437200 | tf_op jit(solution)/shard_map/all_gather | solution.py:103
  577.4 10.3 %convolution_convert_fusion.2 = bf16[512,1536]{1,0:T(8,128)(2,1)} fusion(bf16[512,3072]{1,0:T(8,128)(2,1)} %fusion.31, bf16[3072,1536]{1,0:T(8,128)(2,1)} %all-gather.4.cloned.1.call-done), kind=kOutput, calls=%fused_computation.37 | convolution fusion | flops 4832624640 | bytes 14155776 | tf_op jit(solution)/shard_map/dot_general | solution.py:31
  587.7 2.6 copy.48
  590.3 21.3 %all-to-all-start.2 = ((bf16[512,4,384]{0,2,1:T(8,128)(2,1)}), bf16[512,4,384]{0,2,1:T(8,128)(2,1)}, u32[]{:S(2)}, u32[]{:S(2)}) async-start(bf16[512,4,384]{0,2,1:T(8,128)(2,1)} %bitcast.91), calls=%async_computation.2 | async-start | bytes 3145728 | tf_op jit(solution)/shard_map/all_to_all | solution.py:109
  611.5 22.4 %all_gather.21 = s32[1,2048]{1,0:T(1,128)S(1)} all-gather(s32[1,512]{1,0:T(1,128)S(1)} %copy-done.3), channel_id=1, replica_groups=mesh['dp'=32,'seq'=4] {'seq'}, dimensions={1}, use_global_device_ids=true | all-gather | bytes 10240 | tf_op jit(solution)/shard_map/all_gather | solution.py:117
  636.9 2.8 reshape.135
  645.2 76.6 %while.10 = (s32[]{:T(128)}, bf16[4,512,384]{1,2,0:T(8,128)(2,1)}, s32[4,512]{1,0:T(4,128)S(1)}, s32[1,2048]{1,0:T(1,128)S(1)}, bf16[4,512,3,128]{1,3,2,0:T(8,12...) while((s32[]{:T(128)}, bf16[4,512,384]{1,2,0:T(8,128)(2,1)}, ...), condition=%wide.region_12.13_spmd, body=%wide.region_9.12_spmd.sunk | while | flops 1630734336 | bytes 32009304 | solution.py:65
  645.9 10.4 %fusion.70 = (f32[3,512]{1,0:T(4,128)S(1)}, f32[3,512,2048]{2,1,0:T(8,128)}) fusion(pred[512,2048]{1,0:T(8,128)(4,1)S(1)} %broadcast_compare_fusion.2, bf16[2048,3,128]{2,0,1:T(8,128)(2,1)S(1)} %get-tuple-element.157, bf16[4,512,3,128]{1,3,2,0:T(8,128)(2,1)} %get-tuple-element.156, s32[]{:T(128)} %get-tuple-element.144), kind=kOutput, calls=%fused_computation.73.clone.1 | convolution fusion | flops 817891328 | bytes 15604224 | tf_op jit(solution)/shard_map/while/body/eval_jaxpr/sub | solution.py:57
  656.3 7.3 fusion.71
  665.0 10.4 %fusion.70 = (f32[3,512]{1,0:T(4,128)S(1)}, f32[3,512,2048]{2,1,0:T(8,128)}) fusion(pred[512,2048]{1,0:T(8,128)(4,1)S(1)} %broadcast_compare_fusion.2, bf16[2048,3,128]{2,0,1:T(8,128)(2,1)S(1)} %get-tuple-element.157, bf16[4,512,3,128]{1,3,2,0:T(8,128)(2,1)} %get-tuple-element.156, s32[]{:T(128)} %get-tuple-element.144), kind=kOutput, calls=%fused_computation.73.clone.1 | convolution fusion | flops 817891328 | bytes 15604224 | tf_op jit(solution)/shard_map/while/body/eval_jaxpr/sub | solution.py:57
  675.5 7.3 fusion.71
  684.2 10.4 %fusion.70 = (f32[3,512]{1,0:T(4,128)S(1)}, f32[3,512,2048]{2,1,0:T(8,128)}) fusion(pred[512,2048]{1,0:T(8,128)(4,1)S(1)} %broadcast_compare_fusion.2, bf16[2048,3,128]{2,0,1:T(8,128)(2,1)S(1)} %get-tuple-element.157, bf16[4,512,3,128]{1,3,2,0:T(8,128)(2,1)} %get-tuple-element.156, s32[]{:T(128)} %get-tuple-element.144), kind=kOutput, calls=%fused_computation.73.clone.1 | convolution fusion | flops 817891328 | bytes 15604224 | tf_op jit(solution)/shard_map/while/body/eval_jaxpr/sub | solution.py:57
  694.6 7.3 fusion.71
  703.3 10.4 %fusion.70 = (f32[3,512]{1,0:T(4,128)S(1)}, f32[3,512,2048]{2,1,0:T(8,128)}) fusion(pred[512,2048]{1,0:T(8,128)(4,1)S(1)} %broadcast_compare_fusion.2, bf16[2048,3,128]{2,0,1:T(8,128)(2,1)S(1)} %get-tuple-element.157, bf16[4,512,3,128]{1,3,2,0:T(8,128)(2,1)} %get-tuple-element.156, s32[]{:T(128)} %get-tuple-element.144), kind=kOutput, calls=%fused_computation.73.clone.1 | convolution fusion | flops 817891328 | bytes 15604224 | tf_op jit(solution)/shard_map/while/body/eval_jaxpr/sub | solution.py:57
  713.8 7.3 fusion.71
  721.8 24.4 %all_to_all.88 = bf16[4,512,384]{1,2,0:T(8,128)(2,1)S(1)} all-to-all(bf16[4,512,384]{1,2,0:T(8,128)(2,1)} %get-tuple-element.42), channel_id=1, replica_groups=mesh['dp'=32,'seq'=4] {'seq'}, dimensions={0} | all-to-all | bytes 3145728 | tf_op jit(solution)/shard_map/all_to_all | solution.py:119
  (61 shorter events, 26.9 us)
Async XLA Ops:
  6.5 60.0 %copy-start = (bf16[16,6144]{1,0:T(8,128)(2,1)S(1)}, bf16[16,6144]{1,0:T(8,128)(2,1)}, u32[]{:S(2)}) copy-start(bf16[16,6144]{1,0:T(8,128)(2,1)} %param.14) | copy-start | bytes 589828
  6.5 215.4 %all-gather.6.cloned.1.call-start = ((), (), s32[]{:S(2)}) async-start(), calls=%async_computation.7 | async-start | bytes 9732096 | tf_op jit(solution)/shard_map/all_gather | solution.py:104
  17.1 382.2 %all-gather.8.cloned.1.call-start = ((), (), s32[]{:S(2)}) async-start(), calls=%async_computation.8 | async-start | bytes 9732096 | tf_op jit(solution)/shard_map/all_gather | solution.py:105
  25.7 551.8 %all-gather.4.cloned.1.call-start = ((), (), s32[]{:S(2)}) async-start(), calls=%async_computation.6 | async-start | bytes 9732096 | tf_op jit(solution)/shard_map/all_gather | solution.py:103
  41.0 17.2 %all-to-all-start = ((s32[32,24,1]{1,2,0:T(1,128)}), s32[32,24,1]{1,2,0:T(1,128)S(1)}, u32[]{:S(2)}, u32[]{:S(2)}) async-start(s32[32,24,1]{1,2,0:T(1,128)} %bitcast.7), calls=%async_computation | async-start | bytes 32768 | tf_op jit(solution)/shard_map/all_to_all | solution.py:89
  58.2 8.2 %copy-start.3 = (s32[1,512]{1,0:T(1,128)S(1)}, s32[1,512]{1,0:T(1,128)}, u32[]{:S(2)}) copy-start(s32[1,512]{1,0:T(1,128)} %param.12) | copy-start | bytes 6148
  58.2 8.2 %copy-start.4 = (s32[1,8]{1,0:T(1,128)S(1)}, s32[1,8]{1,0:T(1,128)}, u32[]{:S(2)}) copy-start(s32[1,8]{1,0:T(1,128)} %param.13) | copy-start | bytes 100
  58.2 101.9 %all-to-all-start.1 = ((bf16[32,24,3072]{2,1,0:T(8,128)(2,1)}), bf16[32,24,3072]{2,1,0:T(8,128)(2,1)}, u32[]{:S(2)}, u32[]{:S(2)}) async-start(bf16[32,24,3072]{2,1,0:T(8,128)(2,1)} %bitcast.87), calls=%async_computation.1 | async-start | bytes 9437184 | tf_op jit(solution)/shard_map/all_to_all | solution.py:88
  232.9 177.1 %all-to-all-start.3 = ((bf16[512,4,384]{0,2,1:T(8,128)(2,1)}), bf16[512,4,384]{0,2,1:T(8,128)(2,1)S(1)}, u32[]{:S(2)}, u32[]{:S(2)}) async-start(bf16[512,4,384]{0,2,1:T(8,128)(2,1)} %bitcast.15), calls=%async_computation.3 | async-start | bytes 3145728 | tf_op jit(solution)/shard_map/all_to_all | solution.py:112
  410.0 180.3 %all-to-all-start.4 = ((bf16[512,4,384]{2,0,1:T(8,128)(2,1)}), bf16[512,4,384]{2,0,1:T(8,128)(2,1)S(1)}, u32[]{:S(2)}, u32[]{:S(2)}) async-start(bf16[512,4,384]{2,0,1:T(8,128)(2,1)} %bitcast.92), calls=%async_computation.4 | async-start | bytes 3145728 | tf_op jit(solution)/shard_map/all_to_all | solution.py:113
  590.3 54.9 %all-to-all-start.2 = ((bf16[512,4,384]{0,2,1:T(8,128)(2,1)}), bf16[512,4,384]{0,2,1:T(8,128)(2,1)}, u32[]{:S(2)}, u32[]{:S(2)}) async-start(bf16[512,4,384]{0,2,1:T(8,128)(2,1)} %bitcast.91), calls=%async_computation.2 | async-start | bytes 3145728 | tf_op jit(solution)/shard_map/all_to_all | solution.py:109
  642.8 2.4 copy-start.2
  721.8 26.0 %copy-start.1 = (bf16[16,6144]{1,0:T(8,128)(2,1)S(1)}, bf16[16,6144]{1,0:T(8,128)(2,1)}, u32[]{:S(2)}) copy-start(bf16[16,6144]{1,0:T(8,128)(2,1)} %param.14) | copy-start | bytes 589828
Sparse Core Ops, SparseCore 0:
  17.2 204.6 all-gather.5
  223.6 175.6 all-gather.7
  400.9 176.4 all-gather.3
where the time goes:
time: 762 us; the launch traced here: 755 us
  waiting for transfers between devices  420 us (55%)
  matrix products  106 us (14%)
  starting transfers between devices  79.2 us (10%)
  blocking collectives  75.6 us (10%)
  local copies, waits for them, and re-layouts  45.5 us (6%)
  other arithmetic  14.5 us (2%)
  between operations  13.7 us (2%)
    all_gather x1, waiting for transfers between devices, on_device(): lax.all_gather(columns_full[2], 'dp', axis=0, tiled=True)  147 us
    all_gather x1, waiting for transfers between devices, on_device(): lax.all_gather(columns_full[0], 'dp', axis=0, tiled=True)  145 us
    all_to_all x1, waiting for transfers between devices, on_device(): lax.all_to_all(outgoing, 'dp', split_axis=0, concat_axis=0, tiled=True)  85.9 us
    sub x4, matrix products, attend_block(): exponent = jnp.exp(scores - row_max)  41.7 us
    all_gather x1, waiting for transfers between devices, on_device(): lax.all_gather(columns_full[1], 'dp', axis=0, tiled=True)  41.6 us
    dot_general x4, matrix products, attend_block(): jnp.einsum('hqk,khd->qhd', weights_bf, value_heads, preferred_element_typ...  29.1 us
    all_to_all x1, blocking collectives, on_device(): lax.all_to_all(head_output, 'seq', split_axis=0, concat_axis=1, tiled=True)  24.4 us
    all_gather x1, blocking collectives, on_device(): sequence_clips = lax.all_gather(segment_ids, 'seq', axis=1, tiled=True)[0]  22.4 us
  transfers between devices with their start and end apart: 8, of which 4 were waited for; matrix products, arithmetic and copies ran while one was open for 12% of the time, Pallas kernels for 0%

commit v1 on v0

v1 whole, which is shorter than its diff:
```python
import functools

import jax
import jax.numpy as jnp
from jax import lax
from jax.experimental import pallas as pl
from jax.experimental.pallas import tpu as pltpu
from jax.sharding import PartitionSpec as P

MESH = pl.DeviceIdType.MESH
F32, BF16, I32 = jnp.float32, jnp.bfloat16, jnp.int32
ROWS, WIDTH, HALF, HEAD_DIM = 512, 3072, 1536, 128
BLOCK = WIDTH + HALF + 128
KEY, VALUE, QUERY = 0, 1, 2
PARTS = (
    (KEY, 0, (0, 1, 2)),
    (KEY, 1, (0, 2, 1)),
    (VALUE, 0, (0, 1, 2)),
    (VALUE, 1, (2, 0, 1)),
    (QUERY, 0, (0, 1, 2)),
    (QUERY, 1, (2, 1, 0)),
)


def dot(a, b):
    return jnp.dot(a, b, preferred_element_type=F32)


def dot_nt(a, b):
    return lax.dot_general(a, b, (((1,), (1,)), ((), ())), preferred_element_type=F32)


def iota(shape, dim):
    return lax.broadcasted_iota(I32, shape, dim)


def one_hot(row_ids, lane_ids):
    return jnp.where(row_ids == lane_ids, 1.0, 0.0).astype(BF16)


def project_kernel(
    target, segment, bucket, mod_table, latents, w_query, w_key, w_value,
    q_out, k_out, v_out, seg_out,
    outgoing, incoming, weights, hidden, tags, hits, keys, seg_all,
    a_send, a_recv, w_send, w_recv, s_send, s_recv, x_send, x_recv, h_send, h_recv, f_send, f_recv, local,
):
    me_dp, me_seq = lax.axis_index("dp"), lax.axis_index("seq")
    x_lo, z, y = me_dp // 16, (me_dp // 4) % 4, me_dp % 4
    x_hi, core = me_seq // 2, me_seq % 2
    me = (x_hi * 2 + x_lo, z, y)
    sibling = (me_dp, x_hi * 2 + (1 - core))

    def at_chip(c):
        return ((c[0] % 2) * 16 + c[1] * 4 + c[2], (c[0] // 2) * 2 + core)

    def at_block(b, sign):
        r = (13 * b) % 32
        dz, dy = (r // 4) % 4, r % 4
        return (((x_lo + r // 16) % 2) * 16 + ((z + 4 + sign * dz) % 4) * 4 + (y + 4 + sign * dy) % 4, me_seq)

    def seq_peer(r):
        if r == 1:
            return sibling
        return (me_dp, (1 - x_hi) * 2 + (core if r == 2 else 1 - core))

    barrier = pltpu.get_barrier_semaphore()

    def greet(k, carry):
        pl.semaphore_signal(barrier, inc=1, device_id=((me_dp + k) % 32, me_seq), device_id_type=MESH)
        return carry

    lax.fori_loop(1, 32, greet, 0)
    for peer in (seq_peer(1), seq_peer(2), seq_peer(3), ((1 - x_lo) * 16 + z * 4 + y, (1 - x_hi) * 2 + core)):
        pl.semaphore_signal(barrier, inc=1, device_id=peer, device_id_type=MESH)

    own = []
    for m, shard in ((KEY, w_key), (VALUE, w_value), (QUERY, w_query)):
        copy = pltpu.make_async_copy(shard, weights.at[m, me[0], z, y], local.at[m])
        copy.start()
        own.append(copy)
    seg_all[me_seq] = jnp.broadcast_to(segment[...], (8, ROWS))
    for copy in own:
        copy.wait()
    pl.semaphore_wait(barrier, 35)

    def w_copy(p, phase, pos, off):
        m, half, order = PARTS[p]
        axis, done = order[phase], order[:phase]
        index = [m]
        for ax in range(3):
            index.append(pos % 4 if ax == axis else slice(None) if ax in done else me[ax])
        index.append(pl.ds(48 * half, 48))
        there = list(me)
        there[axis] = (there[axis] + off) % 4
        piece = weights.at[tuple(index)]
        return pltpu.make_async_remote_copy(
            src_ref=piece, dst_ref=piece, send_sem=w_send.at[p, phase, off - 1], recv_sem=w_recv.at[p, phase, off - 1],
            device_id=at_chip(there), device_id_type=MESH,
        )

    def w_start(p, phase):
        axis = PARTS[p][2][phase]
        for off in (1, 3, 2):
            w_copy(p, phase, me[axis], off).start()

    def w_arrived(p, phase):
        axis = PARTS[p][2][phase]
        for off in (1, 3, 2):
            w_copy(p, phase, me[axis] + 4 - off, off).wait_recv()

    for p in range(6):
        w_start(p, 0)

    def s_copy(r, slot):
        return pltpu.make_async_remote_copy(
            src_ref=seg_all.at[slot], dst_ref=seg_all.at[slot], send_sem=s_send.at[r - 1], recv_sem=s_recv.at[r - 1],
            device_id=seq_peer(r), device_id_type=MESH,
        )

    for r in (1, 2, 3):
        s_copy(r, me_seq).start()

    row = target[...] & (ROWS - 1)
    dest = target[...] >> 11
    rel = (((dest >> 4) + x_lo) & 1) * 16 + ((((dest >> 2) & 3) + 4 - z) & 3) * 4 + (((dest & 3) + 4 - y) & 3)
    block = (5 * rel) & 31
    block_hit = jnp.where(iota((32, ROWS), 0) == block, 1.0, 0.0)
    before = one_hot(jnp.minimum(iota((ROWS, ROWS), 0) + 1, iota((ROWS, ROWS), 1)), iota((ROWS, ROWS), 0) + 1)
    earlier = dot(block_hit.astype(BF16), before)
    rank = jnp.sum(block_hit * earlier, axis=0, keepdims=True).astype(I32)
    late = rank >= 16
    keys[0:1] = jnp.where(late, -1, block * 16 + rank)
    keys[1:2] = jnp.where(late, block * 16 + rank - 16, -1)
    keys[2:3] = jnp.where(late, block * 16 + rank - 8, -1)
    token_bucket = jnp.zeros((1, ROWS), I32)
    for clip in range(8):
        token_bucket += jnp.where(segment[...] == clip, bucket[:, clip : clip + 1], 0)
    stacked = jnp.concatenate([row.astype(F32), token_bucket.astype(F32), jnp.zeros((6, ROWS), F32)], axis=0)
    columns = jnp.transpose(stacked)
    row_col, bucket_col = columns[:, 0:1], columns[:, 1:2]
    lane = iota((ROWS, 128), 1)
    hits[...] = jnp.where(bucket_col == lane.astype(F32), 1.0, 0.0).astype(BF16)
    high = jnp.where(row_col >= 256.0, 1.0, 0.0)
    low = row_col - 256.0 * high
    kind = lane % 3
    tag = jnp.where(kind == 0, low, jnp.where(kind == 1, high, 1.0))
    tags[0] = jnp.where(lane < 3, tag, 0.0).astype(BF16)
    tags[1] = jnp.where((lane >= 3) & (lane < 6), tag, 0.0).astype(BF16)

    def pack(c, carry):
        base = pl.multiple_of(c * 128, 128)
        rows = pl.ds(base, 128)
        ids = iota((128, ROWS), 0) + base
        first = one_hot(ids, keys[0:1])
        left = one_hot(ids, keys[1:2])
        right = one_hot(ids, keys[2:3])
        outgoing[rows, 0:WIDTH] = dot(first, latents[...]).astype(BF16)
        outgoing[rows, WIDTH : WIDTH + HALF] = (dot(left, latents[:, 0:HALF]) + dot(right, latents[:, HALF:WIDTH])).astype(BF16)
        outgoing[rows, WIDTH + HALF : BLOCK] = (dot(first, tags[0]) + dot(left + right, tags[1])).astype(BF16)
        return carry

    lax.fori_loop(0, 4, pack, 0)

    for p in range(6):
        w_arrived(p, 0)
        w_start(p, 1)

    def a_copy(b, sign):
        rows = pl.ds(pl.multiple_of(b * 16, 16), 16)
        return pltpu.make_async_remote_copy(
            src_ref=outgoing.at[rows], dst_ref=incoming.at[rows], send_sem=a_send.at[b], recv_sem=a_recv.at[b],
            device_id=at_block(b, sign), device_id_type=MESH,
        )

    def a_start(b, carry):
        a_copy(b, 1).start()
        return carry

    def a_wait(b, carry):
        a_copy(b, -1).wait()
        return carry

    lax.fori_loop(1, 32, a_start, 0)
    incoming[0:16] = outgoing[0:16]
    for p in range(6):
        w_arrived(p, 1)
        w_start(p, 2)
    lax.fori_loop(1, 32, a_wait, 0)

    own_slot, sib_slot, halo_slot = x_hi + core, x_hi + 1 - core, 2 - 2 * x_hi
    pick_lane = iota((8, 128), 1)
    pick_row = iota((8, 128), 0)
    pick_kind = pick_lane - 3 * pick_row
    pick = jnp.where(
        pick_row < 2,
        jnp.where(pick_kind == 0, 1.0, jnp.where(pick_kind == 1, 256.0, jnp.where(pick_kind == 2, 512.0, 0.0))),
        0.0,
    ).astype(BF16)
    rows_in = dot_nt(pick, incoming[:, WIDTH + HALF : BLOCK]).astype(I32) - 512
    odd = (iota((1, ROWS), 1) & 15) >= 8
    keys[0:1] = rows_in[0:1]
    keys[1:2] = jnp.where(odd, -1, rows_in[1:2])
    keys[2:3] = jnp.where(odd, rows_in[1:2], -1)

    def chunk(slot, c):
        return hidden.at[slot, pl.ds(pl.multiple_of(c * 128, 128), 128)]

    def x_copy(slot, c):
        return pltpu.make_async_remote_copy(
            src_ref=chunk(slot, c), dst_ref=chunk(slot, c), send_sem=x_send.at[c], recv_sem=x_recv.at[c],
            device_id=sibling, device_id_type=MESH,
        )

    def h_copy(c):
        return pltpu.make_async_remote_copy(
            src_ref=chunk(own_slot, c), dst_ref=chunk(2 * x_hi, c), send_sem=h_send.at[c], recv_sem=h_recv.at[c % 2],
            device_id=(me_dp, (1 - x_hi) * 2 + c // 2), device_id_type=MESH,
        )

    def f_copy(i, owner):
        c = 2 * owner + i
        return pltpu.make_async_remote_copy(
            src_ref=chunk(halo_slot, c), dst_ref=chunk(halo_slot, c), send_sem=f_send.at[i], recv_sem=f_recv.at[i],
            device_id=sibling, device_id_type=MESH,
        )

    on_edge = x_hi + core == 1

    def place(c, carry):
        base = pl.multiple_of(c * 128, 128)
        rows = pl.ds(base, 128)
        ids = iota((128, ROWS), 0) + base
        whole = dot(one_hot(ids, keys[0:1]), incoming[:, 0:WIDTH])
        left = dot(one_hot(ids, keys[1:2]), incoming[:, WIDTH : WIDTH + HALF])
        right = dot(one_hot(ids, keys[2:3]), incoming[:, WIDTH : WIDTH + HALF])
        placed = whole + jnp.concatenate([left, right], axis=1)
        centered = placed - jnp.mean(placed, axis=1, keepdims=True)
        var = jnp.mean(centered * centered, axis=1, keepdims=True)
        normalized = centered * lax.rsqrt(var + 1e-6)
        modulation = dot(hits[rows, 0:16], mod_table[...])
        hidden[own_slot, rows] = (normalized * (1.0 + modulation[:, WIDTH:]) + modulation[:, :WIDTH]).astype(BF16)
        x_copy(own_slot, c).start()

        @pl.when(on_edge)
        def _():
            h_copy(c).start()

        return carry

    lax.fori_loop(0, 4, place, 0)

    def project(m, out, slot, out_base):
        def step(s, carry):
            r, h = s // 2, s % 2
            w = weights[m, pl.ds(2 * h, 2)].reshape(WIDTH, 384)
            rows = pl.ds(pl.multiple_of(r * 256, 256), 256)
            result = dot(hidden[slot, rows], w).astype(BF16)
            out[pl.ds(pl.multiple_of(out_base + r * 256, 256), 256), pl.ds(pl.multiple_of(h * 384, 128), 384)] = result
            return carry

        lax.fori_loop(0, 4, step, 0)

    for p in (0, 1):
        w_arrived(p, 2)
    project(KEY, k_out, own_slot, own_slot * 512)
    for c in range(4):
        x_copy(sib_slot, c).wait_recv()
    project(KEY, k_out, sib_slot, sib_slot * 512)
    for i in range(2):
        h_copy(2 * core + i).wait_recv()
        f_copy(i, core).start()
    for p in (2, 3):
        w_arrived(p, 2)
    project(VALUE, v_out, own_slot, own_slot * 512)
    project(VALUE, v_out, sib_slot, sib_slot * 512)
    for i in range(2):
        f_copy(i, 1 - core).wait_recv()
    project(KEY, k_out, halo_slot, halo_slot * 512)
    project(VALUE, v_out, halo_slot, halo_slot * 512)
    for p in (4, 5):
        w_arrived(p, 2)
    project(QUERY, q_out, own_slot, core * 512)
    project(QUERY, q_out, sib_slot, (1 - core) * 512)

    for r in (1, 2, 3):
        s_copy(r, (seq_peer(r)[1])).wait_recv()
    for i in range(3):
        seg_out[:, 512 * i : 512 * i + 512] = seg_all[x_hi + i]

    for r in (1, 2, 3):
        s_copy(r, me_seq).wait_send()
    for p in range(6):
        for phase in range(3):
            for off in (1, 3, 2):
                w_copy(p, phase, me[PARTS[p][2][phase]], off).wait_send()
    for c in range(4):
        x_copy(own_slot, c).wait_send()

    @pl.when(on_edge)
    def _():
        for c in range(4):
            h_copy(c).wait_send()

    for i in range(2):
        f_copy(i, core).wait_send()


def project_tokens(target, segment, bucket, mod_table, latents, w_query, w_key, w_value):
    vmem = pl.BlockSpec(memory_space=pltpu.VMEM)
    anywhere = pl.BlockSpec(memory_space=pl.ANY)
    dma = pltpu.SemaphoreType.DMA
    return pl.pallas_call(
        project_kernel,
        out_shape=(
            jax.ShapeDtypeStruct((2 * ROWS, 768), BF16),
            jax.ShapeDtypeStruct((3 * ROWS, 768), BF16),
            jax.ShapeDtypeStruct((3 * ROWS, 768), BF16),
            jax.ShapeDtypeStruct((8, 3 * ROWS), I32),
        ),
        in_specs=[vmem] * 5 + [anywhere] * 3,
        out_specs=(vmem,) * 4,
        scratch_shapes=[
            pltpu.VMEM((ROWS, BLOCK), BF16),
            pltpu.VMEM((ROWS, BLOCK), BF16),
            pltpu.VMEM((3, 4, 4, 4, 96, 384), BF16),
            pltpu.VMEM((3, ROWS, WIDTH), BF16),
            pltpu.VMEM((2, ROWS, 128), BF16),
            pltpu.VMEM((ROWS, 128), BF16),
            pltpu.VMEM((8, ROWS), I32),
            pltpu.VMEM((4, 8, ROWS), I32),
            dma((32,)), dma((32,)), dma((6, 3, 3)), dma((6, 3, 3)), dma((3,)), dma((3,)),
            dma((4,)), dma((4,)), dma((4,)), dma((2,)), dma((2,)), dma((2,)), dma((3,)),
        ],
        compiler_params=pltpu.CompilerParams(collective_id=0, has_side_effects=True, vmem_limit_bytes=60 * 2**20),
        name="project_tokens",
    )(target, segment, bucket, mod_table, latents, w_query, w_key, w_value)


Q_TILE, K_SPAN = 256, 1280


def attend_kernel(info, q, k, v, seg, out):
    tile = pl.program_id(1)
    base = info[0] * ROWS + tile * Q_TILE
    start = pl.multiple_of(jnp.clip(base - 512, 0, 3 * ROWS - K_SPAN), 128)
    span = pl.ds(start, K_SPAN)
    seg_keys = seg[0:1, span]
    seg_rows = seg[:, pl.ds(pl.multiple_of(base, 128), Q_TILE)]
    seg_query = jnp.transpose(seg_rows.astype(F32))[:, 0:1].astype(I32)
    scores = dot_nt(q[...], k[span]) * HEAD_DIM**-0.5
    scores = jnp.where(seg_query == seg_keys, scores, -1e30)
    weight = jnp.exp(scores - jnp.max(scores, axis=1, keepdims=True))
    total = jnp.sum(weight, axis=1, keepdims=True)
    out[...] = dot((weight / total).astype(BF16), v[span]).astype(BF16)


def attend(info, q, k, v, seg):
    return pl.pallas_call(
        attend_kernel,
        out_shape=jax.ShapeDtypeStruct((2 * ROWS, 768), BF16),
        grid_spec=pltpu.PrefetchScalarGridSpec(
            num_scalar_prefetch=1,
            grid=(6, 2 * ROWS // Q_TILE),
            in_specs=[
                pl.BlockSpec((Q_TILE, HEAD_DIM), lambda h, t, info: (t, h)),
                pl.BlockSpec((3 * ROWS, HEAD_DIM), lambda h, t, info: (0, h)),
                pl.BlockSpec((3 * ROWS, HEAD_DIM), lambda h, t, info: (0, h)),
                pl.BlockSpec((8, 3 * ROWS), lambda h, t, info: (0, 0)),
            ],
            out_specs=pl.BlockSpec((Q_TILE, HEAD_DIM), lambda h, t, info: (t, h)),
        ),
        name="attend",
    )(info, q, k, v, seg)


def exchange_kernel(o, out, landed, local, send, recv):
    me_dp, me_seq = lax.axis_index("dp"), lax.axis_index("seq")
    x_hi, core = me_seq // 2, me_seq % 2
    sibling = (me_dp, x_hi * 2 + (1 - core))
    barrier = pltpu.get_barrier_semaphore()
    pl.semaphore_signal(barrier, inc=1, device_id=sibling, device_id_type=MESH)
    pl.semaphore_wait(barrier, 1)
    there = pl.ds(pl.multiple_of((1 - core) * ROWS, ROWS), ROWS)
    here = pl.ds(pl.multiple_of(core * ROWS, ROWS), ROWS)
    copy = pltpu.make_async_remote_copy(
        src_ref=o.at[there], dst_ref=landed, send_sem=send, recv_sem=recv, device_id=sibling, device_id_type=MESH,
    )
    copy.start()
    for h in range(2):
        out[:, pl.ds(pl.multiple_of(h * 768 + core * 384, 128), 384)] = o[here, 384 * h : 384 * h + 384]
    copy.wait()
    for h in range(2):
        out[:, pl.ds(pl.multiple_of(h * 768 + (1 - core) * 384, 128), 384)] = landed[:, 384 * h : 384 * h + 384]


def exchange(o):
    vmem = pl.BlockSpec(memory_space=pltpu.VMEM)
    return pl.pallas_call(
        exchange_kernel,
        out_shape=jax.ShapeDtypeStruct((ROWS, 2 * 768), BF16),
        in_specs=[vmem],
        out_specs=vmem,
        scratch_shapes=[
            pltpu.VMEM((ROWS, 768), BF16), pltpu.SemaphoreType.DMA, pltpu.SemaphoreType.DMA, pltpu.SemaphoreType.DMA,
        ],
        compiler_params=pltpu.CompilerParams(collective_id=1, has_side_effects=True, vmem_limit_bytes=32 * 2**20),
        name="exchange_heads",
    )(o)


def on_device(latents, target, segment_ids, clip_bucket, mod_table, w_query, w_key, w_value):
    q, k, v, seg = project_tokens(
        target.reshape(1, ROWS), segment_ids, clip_bucket, mod_table, latents, w_query, w_key, w_value
    )
    info = (lax.axis_index("seq") // 2).astype(I32).reshape(1)
    return exchange(attend(info, q, k, v, seg))


def solution(mesh):
    in_specs = (
        P(("dp", "seq"), None),
        P(("dp", "seq")),
        P("dp", "seq"),
        P("dp", None),
        P(),
        P("dp", "seq"),
        P("dp", "seq"),
        P("dp", "seq"),
    )
    out_specs = P(("dp", "seq"), None)
    return jax.shard_map(on_device, mesh=mesh, in_specs=in_specs, out_specs=out_specs, check_vma=False)
```

time: 762 us -> 211 us (0.28)
  waiting for transfers between devices: 420 us -> 0 us
  Pallas kernels: 0 us -> 209 us
  matrix products: 106 us -> 0 us
  starting transfers between devices: 79.2 us -> 0 us
  blocking collectives: 75.6 us -> 0 us
  local copies, waits for them, and re-layouts: 45.5 us -> 2.55 us
  other arithmetic: 14.5 us -> 0 us
  between operations: 13.7 us -> 0.02 us
    all_gather x3 -> x0, waiting for transfers between devices: 334 us -> none  [the longest x1 147 us: on_device(): lax.all_gather(columns_full[2], 'dp', axis=0, tiled=True)]
    pallas_call x0 -> x3, Pallas kernels: none -> 209 us  [the longest x1 178 us: project_tokens(): pl.pallas_call(project_kernel, out_shape=(jax.ShapeDtypeStruct((2 * ROWS,...]
    all_to_all x5 -> x0, waiting for transfers between devices: 85.9 us -> none  [the longest x1 85.9 us: on_device(): lax.all_to_all(outgoing, 'dp', split_axis=0, concat_axis=0, tiled=True)]
    all_to_all x5 -> x0, starting transfers between devices: 79.1 us -> none  [the longest x1 22.3 us: on_device(): lax.all_to_all(value_f.astype(jnp.bfloat16), 'seq', split_axis=1, concat_...]
    dot_general x8 -> x0, matrix products: 64.5 us -> none  [the longest x4 29.1 us: attend_block(): jnp.einsum('hqk,khd->qhd', weights_bf, value_heads, preferred_element_typ...]
    all_gather x4 -> x0, blocking collectives: 51.2 us -> none  [the longest x1 22.4 us: on_device(): sequence_clips = lax.all_gather(segment_ids, 'seq', axis=1, tiled=True)[0]]
    sub x4 -> x0, matrix products: 41.7 us -> none  [attend_block(): exponent = jnp.exp(scores - row_max)]
    all_to_all x1 -> x0, blocking collectives: 24.4 us -> none  [on_device(): lax.all_to_all(head_output, 'seq', split_axis=0, concat_axis=1, tiled=True)]
  transfers between devices with their start and end apart: 8 -> 0, of which waited for: 4 -> 0; matrix products, arithmetic and copies ran while one was open for 12% -> 0% of each run, Pallas kernels for 0% -> 0%
where the time goes in v1:
time: 211 us
  Pallas kernels  209 us (99%)
  local copies, waits for them, and re-layouts  2.55 us (1%)
    pallas_call x1, Pallas kernels, project_tokens(): pl.pallas_call(project_kernel, out_shape=(jax.ShapeDtypeStruct((2 * ROWS,...  178 us
    pallas_call x1, Pallas kernels, attend(): pl.pallas_call(attend_kernel, out_shape=jax.ShapeDtypeStruct((2 * ROWS, 7...  28.2 us

profile of v1, /device:TPU:1, one launch (start us, length us, event | category | flops | bytes accessed | tf_op | source)
XLA Modules:
  0.0 211.1 jit_solution(14451171442823527902)
XLA Ops:
  0.0 178.0 %project_tokens.1 = (bf16[1024,768]{1,0:T(8,128)(2,1)}, bf16[1536,768]{1,0:T(8,128)(2,1)}, bf16[1536,768]{1,0:T(8,128)(2,1)}, s32[8,1536]{1,0:T(8,128)}) custom-call(s32[1,512]{1,0:T(1,128)} %bitcast.2, s32[1,512]{1,0:T(1,128)} %segment.1, s32[1,8]{1,0:T(1,128)} %bucket.1, bf16[16,6144]{1,0:T(8,128)(2,1)} %mod_table.1, bf16[512,3072]{1,0:T(8,128)(2,1)} %latents.1, ...), custom_call_target="tpu_custom_call" | custom-call | tf_op jit(solution)/shard_map/project_tokens/pallas_call | solution.py:312
  178.0 28.2 %attend.1.o = bf16[1024,768]{1,0:T(8,128)(2,1)} custom-call(s32[1]{0:T(128)} %bitcast.info, bf16[1024,768]{1,0:T(8,128)(2,1)} %get-tuple-element.9.q, bf16[1536,768]{1,0:T(8,128)(2,1)} %get-tuple-element.10.k, bf16[1536,768]{1,0:T(8,128)(2,1)} %get-tuple-element.11.v, s32[8,1536]{1,0:T(8,128)} %get-tuple-element.12.seg), custom_call_target="tpu_custom_call" | custom-call | tf_op jit(solution)/shard_map/attend/pallas_call | solution.py:358
  206.1 0.0 copy-start
  206.1 1.4 copy-done
  207.6 2.4 %exchange_heads.1 = bf16[512,1536]{1,0:T(8,128)(2,1)S(1)} custom-call(bf16[1024,768]{1,0:T(8,128)(2,1)S(1)} %copy-done), custom_call_target="tpu_custom_call" | custom-call | tf_op jit(solution)/shard_map/exchange_heads/pallas_call | solution.py:398
  209.9 1.1 copy.10
Async XLA Ops:
  206.1 1.4 copy-start

commit v2 on v1

v2 whole, which is shorter than its diff:
```python
import functools

import jax
import jax.numpy as jnp
from jax import lax
from jax.experimental import pallas as pl
from jax.experimental.pallas import tpu as pltpu
from jax.sharding import PartitionSpec as P

MESH = pl.DeviceIdType.MESH
F32, BF16, I32 = jnp.float32, jnp.bfloat16, jnp.int32
ROWS, WIDTH, HALF, HEAD_DIM = 512, 3072, 1536, 128
BLOCK = WIDTH + HALF + 128
KEY, VALUE, QUERY = 0, 1, 2
Q_TILE, SPANS, LOG2E = 256, (640, 896, 1280), 1.4426950408889634
PARTS = (
    (KEY, 0, 48, (0, 1, 2)),
    (KEY, 48, 48, (0, 2, 1)),
    (VALUE, 0, 48, (0, 1, 2)),
    (VALUE, 48, 48, (0, 2, 1)),
    (QUERY, 0, 32, (1, 2, 0)),
    (QUERY, 32, 32, (0, 1, 2)),
    (QUERY, 64, 32, (0, 2, 1)),
)
FRONT = 2432


def dot(a, b):
    return jnp.dot(a, b, preferred_element_type=F32)


def dot_nt(a, b):
    return lax.dot_general(a, b, (((1,), (1,)), ((), ())), preferred_element_type=F32)


def iota(shape, dim):
    return lax.broadcasted_iota(I32, shape, dim)


def one_hot(row_ids, lane_ids):
    return jnp.where(row_ids == lane_ids, 1.0, 0.0).astype(BF16)


def project_kernel(
    target, segment, bucket, mod_table, latents_in, w_query, w_key, w_value,
    q_out, k_out, v_out, seg_out, info_out,
    latents, q_made, k_made, v_made, outgoing, front, back, incoming, weights, hidden, tags, hits, keys, seg_all,
    z_send, z_recv, p_send, p_recv, w_send, w_recv, s_send, s_recv, x_send, x_recv, h_send, h_recv, f_send, f_recv, o_send, o_recv, o_local, local,
):
    me_dp, me_seq = lax.axis_index("dp"), lax.axis_index("seq")
    x_lo, z, y = me_dp // 16, (me_dp // 4) % 4, me_dp % 4
    x_hi, core = me_seq // 2, me_seq % 2
    me = (x_hi * 2 + x_lo, z, y)
    sibling = (me_dp, x_hi * 2 + (1 - core))

    def at_chip(c):
        return ((c[0] % 2) * 16 + c[1] * 4 + c[2], (c[0] // 2) * 2 + core)

    def along_z(dz):
        return (x_lo * 16 + ((z + dz) % 4) * 4 + y, me_seq)

    def in_plane(b, sign):
        return (((x_lo + b // 4) % 2) * 16 + z * 4 + (y + 4 + sign * (b % 4)) % 4, me_seq)

    def seq_peer(r):
        if r == 1:
            return sibling
        return (me_dp, (1 - x_hi) * 2 + (core if r == 2 else 1 - core))

    barrier = pltpu.get_barrier_semaphore()

    def greet(k, carry):
        pl.semaphore_signal(barrier, inc=1, device_id=((me_dp + k) % 32, me_seq), device_id_type=MESH)
        return carry

    lax.fori_loop(1, 32, greet, 0)
    for peer in (seq_peer(1), seq_peer(2), seq_peer(3), ((1 - x_lo) * 16 + z * 4 + y, (1 - x_hi) * 2 + core)):
        pl.semaphore_signal(barrier, inc=1, device_id=peer, device_id_type=MESH)

    load = pltpu.make_async_copy(latents_in, latents, local.at[3])
    load.start()
    own = []
    for m, shard in ((KEY, w_key), (VALUE, w_value), (QUERY, w_query)):
        copy = pltpu.make_async_copy(shard, weights.at[m, me[0], z, y], local.at[m])
        copy.start()
        own.append(copy)
    seg_all[me_seq] = jnp.broadcast_to(segment[...], (8, ROWS))
    for copy in own:
        copy.wait()
    pl.semaphore_wait(barrier, 35)

    def w_copy(p, phase, pos, off):
        m, first_row, row_count, order = PARTS[p]
        axis, done = order[phase], order[:phase]
        index = [m]
        for ax in range(3):
            index.append(pos % 4 if ax == axis else slice(None) if ax in done else me[ax])
        index.append(pl.ds(first_row, row_count))
        there = list(me)
        there[axis] = (there[axis] + off) % 4
        piece = weights.at[tuple(index)]
        return pltpu.make_async_remote_copy(
            src_ref=piece, dst_ref=piece, send_sem=w_send.at[p, phase, off - 1], recv_sem=w_recv.at[p, phase, off - 1],
            device_id=at_chip(there), device_id_type=MESH,
        )

    def w_start(p, phase, offs=(1, 3, 2)):
        axis = PARTS[p][3][phase]
        for off in offs:
            w_copy(p, phase, me[axis], off).start()

    def w_arrived(p, phase):
        axis = PARTS[p][3][phase]
        for off in (1, 3, 2):
            w_copy(p, phase, me[axis] + 4 - off, off).wait_recv()

    for p in range(len(PARTS)):
        w_start(p, 0)

    def s_copy(r, slot):
        return pltpu.make_async_remote_copy(
            src_ref=seg_all.at[slot], dst_ref=seg_all.at[slot], send_sem=s_send.at[r - 1], recv_sem=s_recv.at[r - 1],
            device_id=seq_peer(r), device_id_type=MESH,
        )

    for r in (1, 2, 3):
        s_copy(r, me_seq).start()

    row = target[...] & (ROWS - 1)
    dest = target[...] >> 11
    block = ((((dest >> 2) & 3) + 4 - z) & 3) * 8 + (((dest >> 4) + x_lo) & 1) * 4 + (((dest & 3) + 4 - y) & 3)
    block_hit = jnp.where(iota((32, ROWS), 0) == block, 1.0, 0.0)
    before = one_hot(jnp.minimum(iota((ROWS, ROWS), 0) + 1, iota((ROWS, ROWS), 1)), iota((ROWS, ROWS), 0) + 1)
    earlier = dot(block_hit.astype(BF16), before)
    rank = jnp.sum(block_hit * earlier, axis=0, keepdims=True).astype(I32)
    late = rank >= 16
    keys[0:1] = jnp.where(late, -1, block * 16 + rank)
    keys[1:2] = jnp.where(late, block * 16 + rank - 16, -1)
    keys[2:3] = jnp.where(late, block * 16 + rank - 8, -1)
    token_bucket = jnp.zeros((1, ROWS), I32)
    for clip in range(8):
        token_bucket += jnp.where(segment[...] == clip, bucket[:, clip : clip + 1], 0)
    stacked = jnp.concatenate([row.astype(F32), token_bucket.astype(F32), jnp.zeros((6, ROWS), F32)], axis=0)
    columns = jnp.transpose(stacked)
    row_col, bucket_col = columns[:, 0:1], columns[:, 1:2]
    lane = iota((ROWS, 128), 1)
    hits[...] = jnp.where(bucket_col == lane.astype(F32), 1.0, 0.0).astype(BF16)
    high = jnp.where(row_col >= 256.0, 1.0, 0.0)
    low = row_col - 256.0 * high
    kind = lane % 3
    tag = jnp.where(kind == 0, low, jnp.where(kind == 1, high, 1.0))
    tags[0] = jnp.where(lane < 3, tag, 0.0).astype(BF16)
    tags[1] = jnp.where((lane >= 3) & (lane < 6), tag, 0.0).astype(BF16)

    fore, aft = pl.ds(0, FRONT), pl.ds(FRONT, BLOCK - FRONT)

    def z_copy(stage, dz, sign):
        if stage == 0:
            src, dst = outgoing.at[dz, :, :, fore], front.at[dz]
        else:
            src, dst = back.at[dz], incoming.at[dz, :, :, aft]
        return pltpu.make_async_remote_copy(
            src_ref=src, dst_ref=dst, send_sem=z_send.at[stage, dz], recv_sem=z_recv.at[stage, dz],
            device_id=along_z(dz if sign > 0 else 4 - dz), device_id_type=MESH,
        )

    def p_copy(stage, b, sign):
        if stage == 0:
            src, dst = outgoing.at[:, b, :, aft], back.at[:, b]
        else:
            src, dst = front.at[:, b], incoming.at[:, b, :, fore]
        return pltpu.make_async_remote_copy(
            src_ref=src, dst_ref=dst, send_sem=p_send.at[stage, b], recv_sem=p_recv.at[stage, b],
            device_id=in_plane(b, sign), device_id_type=MESH,
        )

    z_order, p_order = (1, 3, 2), (1, 4, 3, 5, 2, 7, 6)

    def stay(src, dst, i):
        copy = pltpu.make_async_copy(src, dst, local.at[i])
        copy.start()
        return copy

    def pack(c, carry):
        dz = (c + 1) % 4
        base = dz * 128
        ids = iota((128, ROWS), 0) + base
        first = one_hot(ids, keys[0:1])
        left = one_hot(ids, keys[1:2])
        right = one_hot(ids, keys[2:3])

        def put(lo, hi, value):
            outgoing[dz, :, :, lo:hi] = value.astype(BF16).reshape(8, 16, hi - lo)

        put(0, WIDTH, dot(first, latents[...]))
        put(WIDTH, WIDTH + HALF, dot(left, latents[:, 0:HALF]) + dot(right, latents[:, HALF:WIDTH]))
        put(WIDTH + HALF, BLOCK, dot(first, tags[0]) + dot(left + right, tags[1]))

        @pl.when(c < 3)
        def _():
            z_copy(0, dz, 1).start()

        return carry

    for p in range(len(PARTS)):
        w_arrived(p, 0)
        w_start(p, 1)
    load.wait()
    lax.fori_loop(0, 4, pack, 0)

    for b in p_order:
        p_copy(0, b, 1).start()
    stays = [stay(outgoing.at[0, :, :, fore], front.at[0], 0), stay(outgoing.at[:, 0, :, aft], back.at[:, 0], 1)]
    for r in (1, 2, 3):
        s_copy(r, (seq_peer(r)[1])).wait_recv()
    for i in range(3):
        seg_out[:, 512 * i : 512 * i + 512] = seg_all[x_hi + i]

    window = seg_out[0:1, :]
    info_lane = iota((1, 128), 1)
    for t in range(ROWS // Q_TILE):
        base = pl.multiple_of((x_hi + core) * ROWS + t * Q_TILE, 128)
        ids = seg_out[0:1, pl.ds(base, Q_TILE)]
        first = jnp.sum(jnp.where(window < ids[:, 0:1], 1, 0), axis=1, keepdims=True)
        last = jnp.sum(jnp.where(window <= ids[:, Q_TILE - 1 :], 1, 0), axis=1, keepdims=True)
        info_out[t : t + 1, :] = jnp.where(info_lane == 0, first, jnp.where(info_lane == 1, last, base))

    for copy in stays:
        copy.wait()
    for dz in z_order:
        z_copy(0, dz, -1).wait_recv()
    for b in p_order:
        p_copy(1, b, 1).start()
    for b in p_order:
        p_copy(0, b, -1).wait_recv()
    for dz in z_order:
        z_copy(1, dz, 1).start()
    stays = [stay(front.at[:, 0], incoming.at[:, 0, :, fore], 0), stay(back.at[0], incoming.at[0, :, :, aft], 1)]
    for p in (0, 1):
        w_arrived(p, 1)
        w_start(p, 2, (2,))
    for p in range(2, len(PARTS)):
        w_arrived(p, 1)
    for copy in stays:
        copy.wait()
    for dz in z_order:
        z_copy(1, dz, -1).wait_recv()
    for b in p_order:
        p_copy(1, b, -1).wait_recv()
    for p in (0, 1):
        w_start(p, 2, (1, 3))
        w_start(p + 2, 2, (2,))

    def received(lo, hi):
        return incoming[:, :, :, lo:hi].reshape(ROWS, hi - lo)

    own_slot, sib_slot, halo_slot = x_hi + core, x_hi + 1 - core, 2 - 2 * x_hi
    pick_lane = iota((8, 128), 1)
    pick_row = iota((8, 128), 0)
    pick_kind = pick_lane - 3 * pick_row
    pick = jnp.where(
        pick_row < 2,
        jnp.where(pick_kind == 0, 1.0, jnp.where(pick_kind == 1, 256.0, jnp.where(pick_kind == 2, 512.0, 0.0))),
        0.0,
    ).astype(BF16)
    rows_in = dot_nt(pick, received(WIDTH + HALF, BLOCK)).astype(I32) - 512
    odd = (iota((1, ROWS), 1) & 15) >= 8
    keys[0:1] = rows_in[0:1]
    keys[1:2] = jnp.where(odd, -1, rows_in[1:2])
    keys[2:3] = jnp.where(odd, rows_in[1:2], -1)

    def chunk(slot, c):
        return hidden.at[slot, pl.ds(pl.multiple_of(c * 128, 128), 128)]

    def x_copy(slot, c):
        return pltpu.make_async_remote_copy(
            src_ref=chunk(slot, c), dst_ref=chunk(slot, c), send_sem=x_send.at[c], recv_sem=x_recv.at[c],
            device_id=sibling, device_id_type=MESH,
        )

    def h_copy(c):
        return pltpu.make_async_remote_copy(
            src_ref=chunk(own_slot, c), dst_ref=chunk(2 * x_hi, c), send_sem=h_send.at[c], recv_sem=h_recv.at[c % 2],
            device_id=(me_dp, (1 - x_hi) * 2 + c // 2), device_id_type=MESH,
        )

    def f_copy(i, owner):
        c = 2 * owner + i
        return pltpu.make_async_remote_copy(
            src_ref=chunk(halo_slot, c), dst_ref=chunk(halo_slot, c), send_sem=f_send.at[i], recv_sem=f_recv.at[i],
            device_id=sibling, device_id_type=MESH,
        )

    on_edge = x_hi + core == 1

    def place(c, carry):
        base = pl.multiple_of(c * 128, 128)
        rows = pl.ds(base, 128)
        ids = iota((128, ROWS), 0) + base
        whole = dot(one_hot(ids, keys[0:1]), received(0, WIDTH))
        left = dot(one_hot(ids, keys[1:2]), received(WIDTH, WIDTH + HALF))
        right = dot(one_hot(ids, keys[2:3]), received(WIDTH, WIDTH + HALF))
        placed = whole + jnp.concatenate([left, right], axis=1)
        centered = placed - jnp.mean(placed, axis=1, keepdims=True)
        var = jnp.mean(centered * centered, axis=1, keepdims=True)
        normalized = centered * lax.rsqrt(var + 1e-6)
        modulation = dot(hits[rows, 0:16], mod_table[...])
        hidden[own_slot, rows] = (normalized * (1.0 + modulation[:, WIDTH:]) + modulation[:, :WIDTH]).astype(BF16)
        x_copy(own_slot, c).start()

        @pl.when(on_edge)
        def _():
            h_copy(c).start()

        return carry

    lax.fori_loop(0, 4, place, 0)

    made, outs = (k_made, v_made, q_made), (k_out, v_out, q_out)

    def project(m, slot, at):
        def step(r, carry):
            w = jnp.concatenate([weights[m, 2 * h : 2 * h + 2].reshape(WIDTH, 384) for h in range(2)], axis=1)
            rows = pl.ds(pl.multiple_of(r * 256, 256), 256)
            result = dot(hidden[slot, rows], w).astype(BF16)
            for h in range(2):
                made[m][h, pl.ds(pl.multiple_of(at * ROWS + r * 256, 256), 256)] = result[:, 384 * h : 384 * h + 384]
            return carry

        lax.fori_loop(0, 2, step, 0)

    def o_there(m, at, to, owner):
        return pltpu.make_async_remote_copy(
            src_ref=made[m].at[:, pl.ds(pl.multiple_of(at * ROWS, ROWS), ROWS)],
            dst_ref=outs[m].at[owner, :, pl.ds(pl.multiple_of(to * ROWS, ROWS), ROWS)],
            send_sem=o_send.at[m, to], recv_sem=o_recv.at[m, to], device_id=sibling, device_id_type=MESH,
        )

    def o_here(m, at, to):
        return pltpu.make_async_copy(
            made[m].at[:, pl.ds(pl.multiple_of(at * ROWS, ROWS), ROWS)],
            outs[m].at[core, :, pl.ds(pl.multiple_of(to * ROWS, ROWS), ROWS)],
            o_local.at[m, to],
        )

    def make(m, slot):
        project(m, slot, slot)
        o_there(m, slot, slot, core).start()
        o_here(m, slot, slot).start()

    for p in (0, 1):
        w_arrived(p, 2)
        w_start(p + 2, 2, (1, 3))
    for p in (4, 5, 6):
        w_start(p, 2, (2,))
    make(KEY, own_slot)
    for c in range(4):
        x_copy(sib_slot, c).wait_recv()
    make(KEY, sib_slot)
    for p in (2, 3):
        w_arrived(p, 2)
    for p in (4, 5, 6):
        w_start(p, 2, (1, 3))
    make(VALUE, own_slot)
    make(VALUE, sib_slot)
    for i in range(2):
        h_copy(2 * core + i).wait_recv()
        f_copy(i, core).start()
    for i in range(2):
        f_copy(i, 1 - core).wait_recv()
    make(KEY, halo_slot)
    make(VALUE, halo_slot)
    for p in (4, 5, 6):
        w_arrived(p, 2)
    project(QUERY, sib_slot, 1)
    o_there(QUERY, 1, 0, core).start()
    project(QUERY, own_slot, 0)
    o_here(QUERY, 0, 0).start()

    for m in (KEY, VALUE):
        for slot in range(3):
            o_here(m, slot, slot).wait()
            o_there(m, slot, slot, core).wait_send()
            o_there(m, slot, slot, 1 - core).wait_recv()
    o_here(QUERY, 0, 0).wait()
    o_there(QUERY, 1, 0, core).wait_send()
    o_there(QUERY, 1, 0, 1 - core).wait_recv()

    for r in (1, 2, 3):
        s_copy(r, me_seq).wait_send()
    for stage in (0, 1):
        for dz in z_order:
            z_copy(stage, dz, 1).wait_send()
        for b in p_order:
            p_copy(stage, b, 1).wait_send()
    for p in range(len(PARTS)):
        for phase in range(3):
            for off in (1, 3, 2):
                w_copy(p, phase, me[PARTS[p][3][phase]], off).wait_send()
    for c in range(4):
        x_copy(own_slot, c).wait_send()

    @pl.when(on_edge)
    def _():
        for c in range(4):
            h_copy(c).wait_send()

    for i in range(2):
        f_copy(i, core).wait_send()


def project_tokens(target, segment, bucket, mod_table, latents_in, w_query, w_key, w_value):
    vmem = pl.BlockSpec(memory_space=pltpu.VMEM)
    anywhere = pl.BlockSpec(memory_space=pl.ANY)
    dma = pltpu.SemaphoreType.DMA
    return pl.pallas_call(
        project_kernel,
        out_shape=(
            jax.ShapeDtypeStruct((2, 2, ROWS, 384), BF16),
            jax.ShapeDtypeStruct((2, 2, 3 * ROWS, 384), BF16),
            jax.ShapeDtypeStruct((2, 2, 3 * ROWS, 384), BF16),
            jax.ShapeDtypeStruct((8, 3 * ROWS), I32),
            jax.ShapeDtypeStruct((ROWS // Q_TILE, 128), I32),
        ),
        in_specs=[vmem] * 4 + [anywhere] * 4,
        out_specs=(anywhere,) * 3 + (vmem,) * 2,
        scratch_shapes=[
            pltpu.VMEM((ROWS, WIDTH), BF16),
            pltpu.VMEM((2, 2 * ROWS, 384), BF16),
            pltpu.VMEM((2, 3 * ROWS, 384), BF16),
            pltpu.VMEM((2, 3 * ROWS, 384), BF16),
            pltpu.VMEM((4, 8, 16, BLOCK), BF16),
            pltpu.VMEM((4, 8, 16, FRONT), BF16),
            pltpu.VMEM((4, 8, 16, BLOCK - FRONT), BF16),
            pltpu.VMEM((4, 8, 16, BLOCK), BF16),
            pltpu.VMEM((3, 4, 4, 4, 96, 384), BF16),
            pltpu.VMEM((3, ROWS, WIDTH), BF16),
            pltpu.VMEM((2, ROWS, 128), BF16),
            pltpu.VMEM((ROWS, 128), BF16),
            pltpu.VMEM((8, ROWS), I32),
            pltpu.VMEM((4, 8, ROWS), I32),
            dma((2, 4)), dma((2, 4)), dma((2, 8)), dma((2, 8)), dma((len(PARTS), 3, 3)), dma((len(PARTS), 3, 3)), dma((3,)), dma((3,)),
            dma((4,)), dma((4,)), dma((4,)), dma((2,)), dma((2,)), dma((2,)), dma((3, 3)), dma((3, 3)), dma((3, 3)), dma((4,)),
        ],
        compiler_params=pltpu.CompilerParams(collective_id=0, has_side_effects=True, vmem_limit_bytes=60 * 2**20),
        name="project_tokens",
    )(target, segment, bucket, mod_table, latents_in, w_query, w_key, w_value)


def attend_kernel(info, q, k, v, seg, out):
    tile = pl.program_id(1)
    begin = (info[tile, 0] // 128) * 128
    span = info[tile, 1] - begin
    base = pl.multiple_of(info[tile, 2], 128)
    seg_query = jnp.transpose(seg[:, pl.ds(base, Q_TILE)].astype(F32))[:, 0:1]

    def over(width):
        start = pl.multiple_of(jnp.minimum(begin, 3 * ROWS - width), 128)
        rows = pl.ds(start, width)
        bias = jnp.where(seg_query == seg[0:1, rows].astype(F32), 0.0, -1e30)
        ones = jnp.ones((width, HEAD_DIM), BF16)
        for h in range(3):
            cols = slice(h * HEAD_DIM, (h + 1) * HEAD_DIM)
            scores = dot_nt(q[0, 0, :, cols], k[0, 0, rows, cols]) + bias
            weight = jnp.exp2((scores - jnp.max(scores, axis=1, keepdims=True)) * (HEAD_DIM**-0.5 * LOG2E))
            mixed = dot(weight.astype(BF16), jnp.concatenate([v[0, 0, rows, cols], ones], axis=1))
            out[:, cols] = (mixed[:, :HEAD_DIM] / mixed[:, HEAD_DIM:]).astype(BF16)

    least = -1
    for width in SPANS:
        pl.when((span > least) & (span <= width))(functools.partial(over, width))
        least = width


def attend(info, q, k, v, seg):
    return pl.pallas_call(
        attend_kernel,
        out_shape=jax.ShapeDtypeStruct((ROWS, 1536), BF16),
        grid_spec=pltpu.PrefetchScalarGridSpec(
            num_scalar_prefetch=1,
            grid=(4, ROWS // Q_TILE),
            in_specs=[
                pl.BlockSpec((1, 1, Q_TILE, 384), lambda g, t, info: (g % 2, g // 2, t, 0)),
                pl.BlockSpec((1, 1, 3 * ROWS, 384), lambda g, t, info: (g % 2, g // 2, 0, 0)),
                pl.BlockSpec((1, 1, 3 * ROWS, 384), lambda g, t, info: (g % 2, g // 2, 0, 0)),
                pl.BlockSpec((8, 3 * ROWS), lambda g, t, info: (0, 0)),
            ],
            out_specs=pl.BlockSpec((Q_TILE, 384), lambda g, t, info: (t, g)),
        ),
        compiler_params=pltpu.CompilerParams(vmem_limit_bytes=60 * 2**20),
        name="attend",
    )(info, q, k, v, seg)


def on_device(latents, target, segment_ids, clip_bucket, mod_table, w_query, w_key, w_value):
    q, k, v, seg, info = project_tokens(
        target.reshape(1, ROWS), segment_ids, clip_bucket, mod_table, latents, w_query, w_key, w_value
    )
    return attend(info, q, k, v, seg)


def solution(mesh):
    in_specs = (
        P(("dp", "seq"), None),
        P(("dp", "seq")),
        P("dp", "seq"),
        P("dp", None),
        P(),
        P("dp", "seq"),
        P("dp", "seq"),
        P("dp", "seq"),
    )
    out_specs = P(("dp", "seq"), None)
    return jax.shard_map(on_device, mesh=mesh, in_specs=in_specs, out_specs=out_specs, check_vma=False)
```

time: 211 us -> 191 us (0.905)
  Pallas kernels: 209 us -> 190 us
  local copies, waits for them, and re-layouts: 2.55 us -> 0 us
    pallas_call x3 -> x2, Pallas kernels: 209 us -> 190 us  [the longest x1 172 us: project_tokens(): pl.pallas_call(project_kernel, out_shape=(jax.ShapeDtypeStruct((2, 2, ROW...]
    unnamed x3 -> x0, local copies, waits for them, and re-layouts: 2.55 us -> none
where the time goes in v2:
time: 191 us; the launch traced here: 190 us
  Pallas kernels  190 us (99%)
    pallas_call x1, Pallas kernels, project_tokens(): pl.pallas_call(project_kernel, out_shape=(jax.ShapeDtypeStruct((2, 2, ROW...  172 us
    pallas_call x1, Pallas kernels, attend(): pl.pallas_call(attend_kernel, out_shape=jax.ShapeDtypeStruct((ROWS, 1536)...  18.2 us

profile of v2, /device:TPU:1, one launch (start us, length us, event | category | flops | bytes accessed | tf_op | source)
XLA Modules:
  0.0 190.0 jit_solution(11769497199669983089)
XLA Ops:
  0.0 171.8 %project_tokens.1 = (bf16[2,2,512,384]{3,2,1,0:T(8,128)(2,1)}, bf16[2,2,1536,384]{3,2,1,0:T(8,128)(2,1)}, bf16[2,2,1536,384]{3,2,1,0:T(8,128)(2,1)}, s32[8,1536]{1,0:T(8,128)}, s32[2,128]{1,0:T(2,128)}) custom-call(s32[1,512]{1,0:T(1,128)} %bitcast.1, s32[1,512]{1,0:T(1,128)} %segment.1, s32[1,8]{1,0:T(1,128)} %bucket.1, bf16[16,6144]{1,0:T(8,128)(2,1)} %mod_table.1, ...), custom_call_target="tpu_custom_call" | custom-call | tf_op jit(solution)/shard_map/project_tokens/pallas_call | solution.py:416
  171.8 18.2 %attend.1 = bf16[512,1536]{1,0:T(8,128)(2,1)} custom-call(s32[2,128]{1,0:T(2,128)} %get-tuple-element.10.info, bf16[2,2,512,384]{3,2,1,0:T(8,128)(2,1)} %get-tuple-element.11.q, bf16[2,2,1536,384]{3,2,1,0:T(8,128)(2,1)} %get-tuple-element.12.k, bf16[2,2,1536,384]{3,2,1,0:T(8,128)(2,1)} %get-tuple-element.13.v, s32[8,1536]{1,0:T(8,128)} %get-tuple-element.14.seg), custom_call_target="tpu_custom_call" | custom-call | tf_op jit(solution)/shard_map/attend/pallas_call | solution.py:476

commit v3 on v2

--- a/solution.py
+++ b/solution.py
@@ -12,15 +12,15 @@
 ROWS, WIDTH, HALF, HEAD_DIM = 512, 3072, 1536, 128
 BLOCK = WIDTH + HALF + 128
 KEY, VALUE, QUERY = 0, 1, 2
-Q_TILE, SPANS, LOG2E = 256, (640, 896, 1280), 1.4426950408889634
+Q_TILE, SPANS, LOG2E = 256, (512, 640, 768, 896, 1024, 1280), 1.4426950408889634
 PARTS = (
     (KEY, 0, 48, (0, 1, 2)),
     (KEY, 48, 48, (0, 2, 1)),
     (VALUE, 0, 48, (0, 1, 2)),
     (VALUE, 48, 48, (0, 2, 1)),
-    (QUERY, 0, 32, (1, 2, 0)),
-    (QUERY, 32, 32, (0, 1, 2)),
-    (QUERY, 64, 32, (0, 2, 1)),
+    (QUERY, 0, 48, (1, 2, 0)),
+    (QUERY, 48, 32, (0, 1, 2)),
+    (QUERY, 80, 16, (0, 2, 1)),
 )
 FRONT = 2432
 
@@ -250,6 +250,7 @@
     for p in (0, 1):
         w_start(p, 2, (1, 3))
         w_start(p + 2, 2, (2,))
+    w_start(4, 2)
 
     def received(lo, hi):
         return incoming[:, :, :, lo:hi].reshape(ROWS, hi - lo)
@@ -351,7 +352,7 @@
     for p in (0, 1):
         w_arrived(p, 2)
         w_start(p + 2, 2, (1, 3))
-    for p in (4, 5, 6):
+    for p in (5, 6):
         w_start(p, 2, (2,))
     make(KEY, own_slot)
     for c in range(4):
@@ -359,7 +360,7 @@
     make(KEY, sib_slot)
     for p in (2, 3):
         w_arrived(p, 2)
-    for p in (4, 5, 6):
+    for p in (5, 6):
         w_start(p, 2, (1, 3))
     make(VALUE, own_slot)
     make(VALUE, sib_slot)
@@ -459,12 +460,19 @@
         rows = pl.ds(start, width)
         bias = jnp.where(seg_query == seg[0:1, rows].astype(F32), 0.0, -1e30)
         ones = jnp.ones((width, HEAD_DIM), BF16)
-        for h in range(3):
-            cols = slice(h * HEAD_DIM, (h + 1) * HEAD_DIM)
-            scores = dot_nt(q[0, 0, :, cols], k[0, 0, rows, cols]) + bias
+        heads = [(g, slice(e * HEAD_DIM, (e + 1) * HEAD_DIM)) for g in range(2) for e in range(3)]
+
+        def score(g, cols):
+            return dot_nt(q[g, 0, :, cols], k[g, 0, rows, cols]) + bias
+
+        ready = score(*heads[0])
+        for i, (g, cols) in enumerate(heads):
+            scores = ready
+            if i + 1 < len(heads):
+                ready = score(*heads[i + 1])
             weight = jnp.exp2((scores - jnp.max(scores, axis=1, keepdims=True)) * (HEAD_DIM**-0.5 * LOG2E))
-            mixed = dot(weight.astype(BF16), jnp.concatenate([v[0, 0, rows, cols], ones], axis=1))
-            out[:, cols] = (mixed[:, :HEAD_DIM] / mixed[:, HEAD_DIM:]).astype(BF16)
+            mixed = dot(weight.astype(BF16), jnp.concatenate([v[g, 0, rows, cols], ones], axis=1))
+            out[:, g * 384 + cols.start : g * 384 + cols.stop] = (mixed[:, :HEAD_DIM] / mixed[:, HEAD_DIM:]).astype(BF16)
 
     least = -1
     for width in SPANS:
@@ -478,14 +486,14 @@
         out_shape=jax.ShapeDtypeStruct((ROWS, 1536), BF16),
         grid_spec=pltpu.PrefetchScalarGridSpec(
             num_scalar_prefetch=1,
-            grid=(4, ROWS // Q_TILE),
+            grid=(2, ROWS // Q_TILE),
             in_specs=[
-                pl.BlockSpec((1, 1, Q_TILE, 384), lambda g, t, info: (g % 2, g // 2, t, 0)),
-                pl.BlockSpec((1, 1, 3 * ROWS, 384), lambda g, t, info: (g % 2, g // 2, 0, 0)),
-                pl.BlockSpec((1, 1, 3 * ROWS, 384), lambda g, t, info: (g % 2, g // 2, 0, 0)),
-                pl.BlockSpec((8, 3 * ROWS), lambda g, t, info: (0, 0)),
+                pl.BlockSpec((2, 1, Q_TILE, 384), lambda h, t, info: (0, h, t, 0)),
+                pl.BlockSpec((2, 1, 3 * ROWS, 384), lambda h, t, info: (0, h, 0, 0)),
+                pl.BlockSpec((2, 1, 3 * ROWS, 384), lambda h, t, info: (0, h, 0, 0)),
+                pl.BlockSpec((8, 3 * ROWS), lambda h, t, info: (0, 0)),
             ],
-            out_specs=pl.BlockSpec((Q_TILE, 384), lambda g, t, info: (t, g)),
+            out_specs=pl.BlockSpec((Q_TILE, 768), lambda h, t, info: (t, h)),
         ),
         compiler_params=pltpu.CompilerParams(vmem_limit_bytes=60 * 2**20),
         name="attend",

time: 191 us -> 182 us (0.953)
  Pallas kernels: 190 us -> 182 us
    pallas_call x1, Pallas kernels: 18.2 us -> 13.4 us  [attend(): pl.pallas_call(attend_kernel, out_shape=jax.ShapeDtypeStruct((ROWS, 1536)...]
    pallas_call x1, Pallas kernels: 172 us -> 168 us  [project_tokens(): pl.pallas_call(project_kernel, out_shape=(jax.ShapeDtypeStruct((2, 2, ROW...]
where the time goes in v3:
time: 182 us
  Pallas kernels  182 us (100%)
    pallas_call x1, Pallas kernels, project_tokens(): pl.pallas_call(project_kernel, out_shape=(jax.ShapeDtypeStruct((2, 2, ROW...  168 us
    pallas_call x1, Pallas kernels, attend(): pl.pallas_call(attend_kernel, out_shape=jax.ShapeDtypeStruct((ROWS, 1536)...  13.4 us

profile of v3, /device:TPU:1, one launch (start us, length us, event | category | flops | bytes accessed | tf_op | source)
XLA Modules:
  0.0 181.8 jit_solution(941015849093974218)
XLA Ops:
  0.0 168.4 %project_tokens.1 = (bf16[2,2,512,384]{3,2,1,0:T(8,128)(2,1)}, bf16[2,2,1536,384]{3,2,1,0:T(8,128)(2,1)}, bf16[2,2,1536,384]{3,2,1,0:T(8,128)(2,1)}, s32[8,1536]{1,0:T(8,128)}, s32[2,128]{1,0:T(2,128)}) custom-call(s32[1,512]{1,0:T(1,128)} %bitcast.1, s32[1,512]{1,0:T(1,128)} %segment.1, s32[1,8]{1,0:T(1,128)} %bucket.1, bf16[16,6144]{1,0:T(8,128)(2,1)} %mod_table.1, ...), custom_call_target="tpu_custom_call" | custom-call | tf_op jit(solution)/shard_map/project_tokens/pallas_call | solution.py:417
  168.4 13.4 %attend.1 = bf16[512,1536]{1,0:T(8,128)(2,1)} custom-call(s32[2,128]{1,0:T(2,128)} %get-tuple-element.10.info, bf16[2,2,512,384]{3,2,1,0:T(8,128)(2,1)} %get-tuple-element.11.q, bf16[2,2,1536,384]{3,2,1,0:T(8,128)(2,1)} %get-tuple-element.12.k, bf16[2,2,1536,384]{3,2,1,0:T(8,128)(2,1)} %get-tuple-element.13.v, s32[8,1536]{1,0:T(8,128)} %get-tuple-element.14.seg), custom_call_target="tpu_custom_call" | custom-call | tf_op jit(solution)/shard_map/attend/pallas_call | solution.py:484

commit v4 on v3

--- a/solution.py
+++ b/solution.py
@@ -14,8 +14,8 @@
 KEY, VALUE, QUERY = 0, 1, 2
 Q_TILE, SPANS, LOG2E = 256, (512, 640, 768, 896, 1024, 1280), 1.4426950408889634
 PARTS = (
-    (KEY, 0, 48, (0, 1, 2)),
-    (KEY, 48, 48, (0, 2, 1)),
+    (KEY, 0, 48, (1, 0, 2)),
+    (KEY, 48, 48, (2, 0, 1)),
     (VALUE, 0, 48, (0, 1, 2)),
     (VALUE, 48, 48, (0, 2, 1)),
     (QUERY, 0, 48, (1, 2, 0)),
@@ -85,11 +85,11 @@
         copy.start()
         own.append(copy)
     seg_all[me_seq] = jnp.broadcast_to(segment[...], (8, ROWS))
-    for copy in own:
-        copy.wait()
     pl.semaphore_wait(barrier, 35)
 
-    def w_copy(p, phase, pos, off):
+    shards = {KEY: w_key, VALUE: w_value, QUERY: w_query}
+
+    def w_copy(p, phase, pos, off, sending=True):
         m, first_row, row_count, order = PARTS[p]
         axis, done = order[phase], order[:phase]
         index = [m]
@@ -99,8 +99,9 @@
         there = list(me)
         there[axis] = (there[axis] + off) % 4
         piece = weights.at[tuple(index)]
-        return pltpu.make_async_remote_copy(
-            src_ref=piece, dst_ref=piece, send_sem=w_send.at[p, phase, off - 1], recv_sem=w_recv.at[p, phase, off - 1],
+        source = shards[m].at[pl.ds(first_row, row_count)] if phase == 0 and sending else piece
+        return pltpu.make_async_remote_copy(
+            src_ref=source, dst_ref=piece, send_sem=w_send.at[p, phase, off - 1], recv_sem=w_recv.at[p, phase, off - 1],
             device_id=at_chip(there), device_id_type=MESH,
         )
 
@@ -112,7 +113,7 @@
     def w_arrived(p, phase):
         axis = PARTS[p][3][phase]
         for off in (1, 3, 2):
-            w_copy(p, phase, me[axis] + 4 - off, off).wait_recv()
+            w_copy(p, phase, me[axis] + 4 - off, off, False).wait_recv()
 
     for p in range(len(PARTS)):
         w_start(p, 0)
@@ -202,6 +203,8 @@
 
         return carry
 
+    for copy in own:
+        copy.wait()
     for p in range(len(PARTS)):
         w_arrived(p, 0)
         w_start(p, 1)

time: 182 us -> 176 us (0.967)
  Pallas kernels: 182 us -> 176 us
    pallas_call x1, Pallas kernels: 168 us -> 163 us  [project_tokens(): pl.pallas_call(project_kernel, out_shape=(jax.ShapeDtypeStruct((2, 2, ROW...]
where the time goes in v4:
time: 176 us
  Pallas kernels  176 us (100%)
    pallas_call x1, Pallas kernels, project_tokens(): pl.pallas_call(project_kernel, out_shape=(jax.ShapeDtypeStruct((2, 2, ROW...  163 us
    pallas_call x1, Pallas kernels, attend(): pl.pallas_call(attend_kernel, out_shape=jax.ShapeDtypeStruct((ROWS, 1536)...  13.4 us

profile of v4, /device:TPU:1, one launch (start us, length us, event | category | flops | bytes accessed | tf_op | source)
XLA Modules:
  0.0 176.2 jit_solution(3258727595198811236)
XLA Ops:
  0.0 162.8 %project_tokens.1 = (bf16[2,2,512,384]{3,2,1,0:T(8,128)(2,1)}, bf16[2,2,1536,384]{3,2,1,0:T(8,128)(2,1)}, bf16[2,2,1536,384]{3,2,1,0:T(8,128)(2,1)}, s32[8,1536]{1,0:T(8,128)}, s32[2,128]{1,0:T(2,128)}) custom-call(s32[1,512]{1,0:T(1,128)} %bitcast.1, s32[1,512]{1,0:T(1,128)} %segment.1, s32[1,8]{1,0:T(1,128)} %bucket.1, bf16[16,6144]{1,0:T(8,128)(2,1)} %mod_table.1, ...), custom_call_target="tpu_custom_call" | custom-call | tf_op jit(solution)/shard_map/project_tokens/pallas_call | solution.py:420
  162.8 13.4 %attend.1 = bf16[512,1536]{1,0:T(8,128)(2,1)} custom-call(s32[2,128]{1,0:T(2,128)} %get-tuple-element.10.info, bf16[2,2,512,384]{3,2,1,0:T(8,128)(2,1)} %get-tuple-element.11.q, bf16[2,2,1536,384]{3,2,1,0:T(8,128)(2,1)} %get-tuple-element.12.k, bf16[2,2,1536,384]{3,2,1,0:T(8,128)(2,1)} %get-tuple-element.13.v, s32[8,1536]{1,0:T(8,128)} %get-tuple-element.14.seg), custom_call_target="tpu_custom_call" | custom-call | tf_op jit(solution)/shard_map/attend/pallas_call | solution.py:487

commit v5 on v4

--- a/solution.py
+++ b/solution.py
@@ -356,15 +356,13 @@
         w_arrived(p, 2)
         w_start(p + 2, 2, (1, 3))
     for p in (5, 6):
-        w_start(p, 2, (2,))
+        w_start(p, 2)
     make(KEY, own_slot)
     for c in range(4):
         x_copy(sib_slot, c).wait_recv()
     make(KEY, sib_slot)
     for p in (2, 3):
         w_arrived(p, 2)
-    for p in (5, 6):
-        w_start(p, 2, (1, 3))
     make(VALUE, own_slot)
     make(VALUE, sib_slot)
     for i in range(2):

time: 176 us -> 174 us (0.989)
  Pallas kernels: 176 us -> 174 us
where the time goes in v5:
time: 174 us
  Pallas kernels  174 us (100%)
    pallas_call x1, Pallas kernels, project_tokens(): pl.pallas_call(project_kernel, out_shape=(jax.ShapeDtypeStruct((2, 2, ROW...  161 us
    pallas_call x1, Pallas kernels, attend(): pl.pallas_call(attend_kernel, out_shape=jax.ShapeDtypeStruct((ROWS, 1536)...  12.5 us

profile of v5, /device:TPU:1, one launch (start us, length us, event | category | flops | bytes accessed | tf_op | source)
XLA Modules:
  0.0 173.7 jit_solution(11028747650076544501)
XLA Ops:
  0.0 161.2 %project_tokens.1 = (bf16[2,2,512,384]{3,2,1,0:T(8,128)(2,1)}, bf16[2,2,1536,384]{3,2,1,0:T(8,128)(2,1)}, bf16[2,2,1536,384]{3,2,1,0:T(8,128)(2,1)}, s32[8,1536]{1,0:T(8,128)}, s32[2,128]{1,0:T(2,128)}) custom-call(s32[1,512]{1,0:T(1,128)} %bitcast.1, s32[1,512]{1,0:T(1,128)} %segment.1, s32[1,8]{1,0:T(1,128)} %bucket.1, bf16[16,6144]{1,0:T(8,128)(2,1)} %mod_table.1, ...), custom_call_target="tpu_custom_call" | custom-call | tf_op jit(solution)/shard_map/project_tokens/pallas_call | solution.py:418
  161.2 12.5 %attend.1 = bf16[512,1536]{1,0:T(8,128)(2,1)} custom-call(s32[2,128]{1,0:T(2,128)} %get-tuple-element.10.info, bf16[2,2,512,384]{3,2,1,0:T(8,128)(2,1)} %get-tuple-element.11.q, bf16[2,2,1536,384]{3,2,1,0:T(8,128)(2,1)} %get-tuple-element.12.k, bf16[2,2,1536,384]{3,2,1,0:T(8,128)(2,1)} %get-tuple-element.13.v, s32[8,1536]{1,0:T(8,128)} %get-tuple-element.14.seg), custom_call_target="tpu_custom_call" | custom-call | tf_op jit(solution)/shard_map/attend/pallas_call | solution.py:485
